TPU v7x, 32 devices: a whole 2x2x4 slice. The times are simulated.
32 devices in a mesh: cuts: 8 (over z, y), angle: 4 (over x, core).
Axes of the slice: x: 2, y: 2, z: 4, core: 2. Of those that a mesh axis runs over, the one named last changes fastest.
Arguments:
- density: bfloat16 [8, 576, 256], P('cuts', 'angle'), may hold values from 0.049804688 to 2
- kernel_blocks: bfloat16 [576, 256, 384], P('cuts'), may hold values from -0.015625 to 0.015625
Outputs:
- sinogram: bfloat16 [8, 576, 384], P('cuts', 'angle')
All inputs are finite; a program needn't handle non-finite values.
Results may differ from a plain program's by a relative error of at most 0.0012.
Values may be sent and summed in bfloat16 or wider, within the bound.
A program may use at most 128 MiB of HBM per device.

v0:
```python
import jax
import jax.numpy as jnp
from jax import lax
from jax.sharding import PartitionSpec as P


def local(density, kernel_blocks):
    angles_dev = density.shape[1]
    offsets_dev = kernel_blocks.shape[0]
    angle_count = lax.axis_size("angle")
    offset_start = lax.axis_index("cuts") * offsets_dev
    block_steps = offset_start // angles_dev
    remainder = offset_start - block_steps * angles_dev
    gathered = lax.all_gather(density, "cuts", axis=0, tiled=True)
    full_cycle = lax.all_gather(gathered, "angle", axis=1, tiled=True)
    doubled = jnp.concatenate([full_cycle, full_cycle[:, :angles_dev]], axis=1)
    window_start = (lax.axis_index("angle") - block_steps - 1) % angle_count * angles_dev
    window = lax.dynamic_slice_in_dim(doubled, window_start, 2 * angles_dev, 1)

    def shifted_rows(offset_lag):
        return lax.dynamic_slice_in_dim(window, angles_dev - remainder - offset_lag, angles_dev, 1)

    offset_lags = jnp.arange(offsets_dev, dtype=jnp.int32)
    stacked = jax.vmap(shifted_rows)(offset_lags)
    contribution = lax.psum_scatter(
        jnp.einsum("lsvr,lrb->svb", stacked, kernel_blocks, preferred_element_type=jnp.float32),
        "cuts",
        scatter_dimension=0,
        tiled=True,
    )
    return contribution.astype(jnp.bfloat16)


def solution(mesh):
    return jax.shard_map(
        local,
        mesh=mesh,
        in_specs=(P("cuts", "angle", None), P("cuts", None, None)),
        out_specs=P("cuts", "angle", None),
        check_vma=False,
    )
```

profile of v0, /device:TPU:0, one launch (start us, length us, event | category | flops | bytes accessed | tf_op | source)
XLA Modules:
  0.0 192.4 jit_solution(5741918982668984526)
XLA Ops:
  6.5 0.0 all-gather.2.cloned.1.call-start
  6.5 33.4 %all_gather.6 = bf16[8,144,256]{2,1,0:T(8,128)(2,1)S(1)} all-gather(bf16[1,144,256]{2,1,0:T(8,128)(2,1)} %param.2), channel_id=1, replica_groups=mesh['cuts'=8,'angle'=4] {'cuts'}, dimensions={0}, use_global_device_ids=true | all-gather | bytes 663552 | tf_op jit(solution)/shard_map/all_gather | solution.py:14
  40.0 1.0 copy.5
  41.0 0.0 all-gather.2.cloned.1.call-update
  41.0 0.0 reduce-scatter.2.cloned.1.call-start
  41.1 25.2 %all-gather.2.cloned.1.call-done = bf16[8,576,256]{2,0,1:T(8,128)(2,1)} async-done(((bf16[8,144,256]{2,0,1:T(8,128)(2,1)}), bf16[8,576,256]{2,0,1:T(8,128)(2,1)}) %all-gather.2.cloned.1.call-update) | async-done | bytes 2359312 | tf_op jit(solution)/shard_map/all_gather | solution.py:15
  66.2 1.1 slice.7
  67.3 2.2 %fusion.2 = bf16[8,288,256]{2,0,1:T(8,128)(2,1)S(1)} fusion(s32[]{:T(128)S(6)} %select_n.26, bf16[8,576,256]{2,0,1:T(8,128)(2,1)} %all-gather.2.cloned.1.call-done, bf16[8,144,256]{2,0,1:T(8,128)(2,1)S(1)} %slice.7), kind=kLoop, calls=%fused_computation.6 | loop fusion | flops 589824 | bytes 4128772 | tf_op jit(solution)/shard_map/concatenate | solution.py:16
  69.5 15.8 %gather_fusion = bf16[72,8,144,256]{3,1,2,0:T(8,128)(2,1)} fusion(bf16[8,288,256]{2,0,1:T(8,128)(2,1)S(1)} %fusion.2, s32[72]{0:T(128)S(1)} %fusion.5), kind=kCustom, calls=%fused_computation | custom fusion | bytes 84935520 | tf_op jit(solution)/shard_map/vmap()/gather | solution.py:21
  85.4 30.6 %fusion = f32[8,144,384,1]{2,0,1,3:T(8,128)S(1)} fusion(bf16[72,8,144,256]{3,1,2,0:T(8,128)(2,1)} %gather_fusion, bf16[72,256,384]{2,1,0:T(8,128)(2,1)} %param.3), kind=kOutput, calls=%fused_computation.1 | convolution fusion | flops 16307453952 | bytes 58392576 | tf_op jit(solution)/shard_map/lsvr,lrb->svb/dot_general | solution.py:26
  116.0 1.6 copy.11
  117.5 0.0 reduce-scatter.2.cloned.1.call-update
  117.6 66.4 %reduce-scatter.2.cloned.1.call-done = f32[1,144,384]{2,1,0:T(8,128)} async-done(((f32[8,144,384]{2,1,0:T(8,128)}), f32[1,144,384]{2,1,0:T(8,128)}) %reduce-scatter.2.cloned.1.call-update) | async-done | bytes 221200 | tf_op jit(solution)/shard_map/reduce_scatter | solution.py:25
  184.0 1.6 convert_element_type.3
  (1 shorter events, 0.0 us)
Async XLA Ops:
  6.5 59.7 %all-gather.2.cloned.1.call-start = ((), (), s32[]{:S(2)}) async-start(), calls=%async_computation.1 | async-start | bytes 2949120 | tf_op jit(solution)/shard_map/all_gather | solution.py:15
  41.0 143.0 %reduce-scatter.2.cloned.1.call-start = ((), (), s32[]{:S(2)}) async-start(), calls=%async_computation.2 | async-start | bytes 1990656 | tf_op jit(solution)/shard_map/reduce_scatter | solution.py:25
Sparse Core Ops, SparseCore 0:
  41.1 25.0 all-gather.1
  117.7 66.2 reduce-scatter.1
where the time goes:
time: 193 us; the launch traced here: 192 us
  waiting for transfers between devices  91.6 us (47%)
  blocking collectives  33.4 us (17%)
  matrix products  30.6 us (16%)
  local copies, waits for them, and re-layouts  19.5 us (10%)
  between operations  13.5 us (7%)
  other arithmetic  3.77 us (2%)
    reduce_scatter x1, waiting for transfers between devices, local(): lax.psum_scatter(jnp.einsum('lsvr,lrb->svb', stacked, kernel_blocks, pref...  66.4 us
    all_gather x1, blocking collectives, local(): gathered = lax.all_gather(density, 'cuts', axis=0, tiled=True)  33.4 us
    dot_general x1, matrix products, local(): jnp.einsum('lsvr,lrb->svb', stacked, kernel_blocks, preferred_element_typ...  30.6 us
    all_gather x1, waiting for transfers between devices, local(): full_cycle = lax.all_gather(gathered, 'angle', axis=1, tiled=True)  25.2 us
    gather x1, local copies, waits for them, and re-layouts, shifted_rows(): lax.dynamic_slice_in_dim(window, angles_dev - remainder - offset_lag, ang...  15.8 us
  transfers between devices with their start and end apart: 2, of which 2 were waited for; matrix products, arithmetic and copies ran while one was open for 0% of the time, Pallas kernels for 0%

commit v1 on v0

v1 whole, which is shorter than its diff:
```python
import functools
import jax
import jax.numpy as jnp
from jax import lax
from jax.experimental import pallas as pl
from jax.experimental.pallas import tpu as pltpu
from jax.sharding import PartitionSpec as P

MESH = pl.DeviceIdType.MESH


def split_of(count, options):
    for n in options:
        if count % n == 0:
            return n
    return 1


def project_kernel(cuts, views, offsets, slices, group, chunk, w_ref, k_ref, out_ref,
                   k_buf, acc, tmp, part, y_recv, z_recv,
                   k_sem, ys_sem, yr_sem, zs_sem, zr_sem):
    bins = out_ref.shape[-1]
    slabs = bins // 128
    depth = cuts // 2
    steps = offsets // (2 * group)
    chunks = views // chunk
    rows = (chunk + 2) * slices
    cut = lax.axis_index("cuts")
    ang = lax.axis_index("angle")
    z, y = cut // 2, cut % 2
    first = views - (cut * offsets) % views - 2

    def k_copy(step):
        at = pl.ds(step * 2 * group, 2 * group)
        return pltpu.make_async_copy(k_ref.at[at], k_buf.at[at], k_sem.at[step])

    for step in range(steps):
        k_copy(step).start()

    barrier = pltpu.get_barrier_semaphore()
    pl.semaphore_signal(barrier, inc=1, device_id=(2 * z + 1 - y, ang), device_id_type=MESH)
    for d in range(1, depth):
        pl.semaphore_signal(barrier, inc=1, device_id=(2 * lax.rem(z + d, depth) + y, ang), device_id_type=MESH)
    pl.semaphore_wait(barrier, depth)

    def y_copy(m):
        return pltpu.make_async_remote_copy(
            src_ref=part.at[m, 1 - y], dst_ref=y_recv.at[m],
            send_sem=ys_sem.at[m], recv_sem=yr_sem.at[m],
            device_id=(2 * z + 1 - y, ang), device_id_type=MESH)

    def z_copy(m, d):
        peer = lax.rem(z + d, depth)
        return pltpu.make_async_remote_copy(
            src_ref=part.at[m, y, peer], dst_ref=z_recv.at[m, d - 1],
            send_sem=zs_sem.at[m, d - 1], recv_sem=zr_sem.at[m, d - 1],
            device_id=(2 * peer + y, ang), device_id_type=MESH)

    def z_stage(m):
        y_copy(m).wait_recv()
        part[m, y] += y_recv[m]
        for d in range(depth - 1, 0, -1):
            z_copy(m, d).start()

    for m in range(chunks):
        def body(step, _):
            if m == 0:
                k_copy(step).wait()
            left, right = [], []
            for n in range(group):
                pair = step * group + n
                row = pl.multiple_of((first - 2 * pair + m * chunk) * slices, 16)
                left.append(w_ref[pl.ds(row, rows), :])
                right.append(jnp.concatenate([k_buf[2 * pair], k_buf[2 * pair + 1]], axis=1))
            product = jnp.dot(jnp.concatenate(left, axis=1), jnp.concatenate(right, axis=0),
                              preferred_element_type=jnp.float32)

            @pl.when(step == 0)
            def _():
                acc[...] = product

            @pl.when(step > 0)
            def _():
                acc[...] += product

            return 0

        lax.fori_loop(0, steps, body, 0)
        for b in range(slabs):
            tmp[b] = (acc[slices:slices + chunk * slices, 128 * b:128 * (b + 1)]
                      + acc[:chunk * slices, bins + 128 * b:bins + 128 * (b + 1)])
        for s in range(slices):
            for b in range(slabs):
                part[m, s % 2, s // 2, :, 128 * b:128 * (b + 1)] = tmp[b, pl.ds(s, chunk, stride=slices), :]
        y_copy(m).start()
        if m > 0:
            z_stage(m - 1)
    z_stage(chunks - 1)
    for m in range(chunks):
        total = part[m, y, z]
        for d in range(1, depth):
            z_copy(m, d).wait_recv()
            total += z_recv[m, d - 1]
        out_ref[0, m * chunk:(m + 1) * chunk, :] = total.astype(out_ref.dtype)
    for m in range(chunks):
        y_copy(m).wait_send()
        for d in range(1, depth):
            z_copy(m, d).wait_send()


def project(window, kernel_blocks, cuts, views, slices):
    offsets, radii, bins = kernel_blocks.shape
    group = split_of(offsets // 2, (3, 2))
    chunk = 48 if views % 48 == 0 else views
    chunks, depth = views // chunk, cuts // 2
    rows = (chunk + 2) * slices
    return pl.pallas_call(
        functools.partial(project_kernel, cuts, views, offsets, slices, group, chunk),
        out_shape=jax.ShapeDtypeStruct((1, views, bins), jnp.bfloat16),
        in_specs=[pl.BlockSpec(memory_space=pltpu.VMEM), pl.BlockSpec(memory_space=pl.ANY)],
        out_specs=pl.BlockSpec(memory_space=pltpu.VMEM),
        scratch_shapes=[
            pltpu.VMEM((offsets, radii, bins), jnp.bfloat16),
            pltpu.VMEM((rows, 2 * bins), jnp.float32),
            pltpu.VMEM((bins // 128, chunk * slices, 128), jnp.float32),
            pltpu.VMEM((chunks, 2, depth, chunk, bins), jnp.float32),
            pltpu.VMEM((chunks, depth, chunk, bins), jnp.float32),
            pltpu.VMEM((chunks, depth - 1, chunk, bins), jnp.float32),
            pltpu.SemaphoreType.DMA((offsets // (2 * group),)),
            pltpu.SemaphoreType.DMA((chunks,)),
            pltpu.SemaphoreType.DMA((chunks,)),
            pltpu.SemaphoreType.DMA((chunks, depth - 1)),
            pltpu.SemaphoreType.DMA((chunks, depth - 1)),
        ],
        compiler_params=pltpu.CompilerParams(
            collective_id=0, has_side_effects=True, vmem_limit_bytes=44 * 2**20),
        cost_estimate=pl.CostEstimate(
            flops=2 * views * slices * offsets * radii * bins,
            bytes_accessed=2 * offsets * radii * bins, transcendentals=0),
        name="project",
    )(window, kernel_blocks)


def local(density, kernel_blocks):
    angles_dev = density.shape[1]
    offsets_dev = kernel_blocks.shape[0]
    angle_count = lax.axis_size("angle")
    cuts = lax.axis_size("cuts")
    offset_start = lax.axis_index("cuts") * offsets_dev
    block_steps = offset_start // angles_dev
    gathered = lax.all_gather(density, "cuts", axis=0, tiled=True)
    slices, _, radii = gathered.shape
    full_cycle = lax.all_gather(gathered, "angle", axis=1, tiled=True)
    doubled = jnp.concatenate([full_cycle, full_cycle[:, :angles_dev]], axis=1)
    window_start = (lax.axis_index("angle") - block_steps - 1) % angle_count * angles_dev
    window = lax.dynamic_slice_in_dim(doubled, window_start, 2 * angles_dev, 1)
    rows = jnp.roll(jnp.swapaxes(window, 0, 1), -1, axis=0).reshape(2 * angles_dev * slices, radii)
    return project(rows, kernel_blocks, cuts, angles_dev, slices)


def solution(mesh):
    return jax.shard_map(
        local,
        mesh=mesh,
        in_specs=(P("cuts", "angle", None), P("cuts", None, None)),
        out_specs=P("cuts", "angle", None),
        check_vma=False,
    )
```

time: 193 us -> 127 us (0.66)
  waiting for transfers between devices: 91.6 us -> 25.1 us
  Pallas kernels: 0 us -> 48 us
  matrix products: 30.6 us -> 0 us
  local copies, waits for them, and re-layouts: 19.5 us -> 2.69 us
  blocking collectives: 33.4 us -> 35.6 us
  other arithmetic: 3.77 us -> 1.6 us
    reduce_scatter x1 -> x0, waiting for transfers between devices: 66.4 us -> none  [local(): lax.psum_scatter(jnp.einsum('lsvr,lrb->svb', stacked, kernel_blocks, pref...]
    pallas_call x0 -> x1, Pallas kernels: none -> 48 us  [project(): pl.pallas_call(functools.partial(project_kernel, cuts, views, offsets, sl...]
    dot_general x1 -> x0, matrix products: 30.6 us -> none  [local(): jnp.einsum('lsvr,lrb->svb', stacked, kernel_blocks, preferred_element_typ...]
    gather x1 -> x0, local copies, waits for them, and re-layouts: 15.8 us -> none  [shifted_rows(): lax.dynamic_slice_in_dim(window, angles_dev - remainder - offset_lag, ang...]
    all_gather x1, blocking collectives: 33.4 us -> 35.6 us  [local(): gathered = lax.all_gather(density, 'cuts', axis=0, tiled=True)]
    concatenate x2 -> x1, other arithmetic: 2.18 us -> 0.09 us  [local(): jnp.roll(jnp.swapaxes(window, 0, 1), -1, axis=0)]
  transfers between devices with their start and end apart: 2 -> 1, of which waited for: 2 -> 1; matrix products, arithmetic and copies ran while one was open for 0% -> 0% of each run, Pallas kernels for 0% -> 0%
where the time goes in v1:
time: 127 us
  Pallas kernels  48 us (38%)
  blocking collectives  35.6 us (28%)
  waiting for transfers between devices  25.1 us (20%)
  between operations  13.5 us (11%)
  local copies, waits for them, and re-layouts  2.69 us (2%)
  other arithmetic  1.6 us (1%)
    pallas_call x1, Pallas kernels, project(): pl.pallas_call(functools.partial(project_kernel, cuts, views, offsets, sl...  48 us
    all_gather x1, blocking collectives, local(): gathered = lax.all_gather(density, 'cuts', axis=0, tiled=True)  35.6 us
    all_gather x1, waiting for transfers between devices, local(): full_cycle = lax.all_gather(gathered, 'angle', axis=1, tiled=True)  25.1 us
  transfers between devices with their start and end apart: 1, of which 1 were waited for; matrix products, arithmetic and copies ran while one was open for 0% of the time, Pallas kernels for 0%

profile of v1, /device:TPU:0, one launch (start us, length us, event | category | flops | bytes accessed | tf_op | source)
XLA Modules:
  0.0 126.6 jit_solution(3418768890770185962)
XLA Ops:
  6.5 0.0 all-gather.2.cloned.1.call-start
  6.5 35.6 %all_gather.6 = bf16[8,144,256]{2,1,0:T(8,128)(2,1)} all-gather(bf16[1,144,256]{2,1,0:T(8,128)(2,1)} %param.2), channel_id=1, replica_groups=mesh['cuts'=8,'angle'=4] {'cuts'}, dimensions={0}, use_global_device_ids=true | all-gather | bytes 663552 | tf_op jit(solution)/shard_map/all_gather | solution.py:151
  42.2 0.0 all-gather.2.cloned.1.call-update
  42.2 25.1 %all-gather.2.cloned.1.call-done = bf16[8,576,256]{2,1,0:T(8,128)(2,1)} async-done(((bf16[8,144,256]{2,1,0:T(8,128)(2,1)}), bf16[8,576,256]{2,1,0:T(8,128)(2,1)}) %all-gather.2.cloned.1.call-update) | async-done | bytes 2359312 | tf_op jit(solution)/shard_map/all_gather | solution.py:153
  67.3 1.1 slice.14
  68.4 1.5 %fusion.1 = bf16[288,8,256]{2,0,1:T(8,128)(2,1)S(1)} fusion(s32[]{:T(128)S(6)} %select_n.16, bf16[8,576,256]{2,1,0:T(8,128)(2,1)} %all-gather.2.cloned.1.call-done, bf16[8,144,256]{2,1,0:T(8,128)(2,1)S(1)} %slice.14), kind=kLoop, calls=%fused_computation.3 | loop fusion | flops 2359296 | bytes 4128772 | tf_op jit(solution)/shard_map/transpose | solution.py:157
  70.0 0.3 slice.15
  70.3 0.1 pad_maximum_fusion
  70.4 0.7 copy.6
  71.0 48.0 %project.1 = bf16[1,144,384]{2,1,0:T(8,128)(2,1)S(1)} custom-call(bf16[2304,256]{1,0:T(8,128)(2,1)S(1)} %bitcast.5, bf16[72,256,384]{2,1,0:T(8,128)(2,1)} %k_ref.1), custom_call_target="tpu_custom_call" | custom-call | flops 16307453952 | bytes 14155776 | tf_op jit(solution)/shard_map/project/pallas_call | solution.py:117
  119.1 0.6 copy.8
  (1 shorter events, 0.0 us)
Async XLA Ops:
  6.5 60.8 %all-gather.2.cloned.1.call-start = ((), (), s32[]{:S(2)}) async-start(), calls=%async_computation | async-start | bytes 2949120 | tf_op jit(solution)/shard_map/all_gather | solution.py:153
Sparse Core Ops, SparseCore 0:
  42.3 24.9 all-gather.1

commit v2 on v1

--- a/solution.py
+++ b/solution.py
@@ -141,21 +141,106 @@
     )(window, kernel_blocks)
 
 
+def gather_kernel(cuts, angles, views, offsets, d_ref, out_ref, turn, held,
+                  as_sem, ar_sem, zs_sem, zr_sem, ys_sem, yr_sem):
+    depth = cuts // 2
+    cut = lax.axis_index("cuts")
+    ang = lax.axis_index("angle")
+    z, y = cut // 2, cut % 2
+
+    def z_at(d):
+        return lax.rem(z + d + depth, depth)
+
+    def angle_at(d):
+        return lax.rem(ang + d + angles, angles)
+
+    def block_of(to_z, j):
+        return lax.rem(ang - (2 * to_z * offsets) // views - 1 + j + 2 * angles, angles)
+
+    barrier = pltpu.get_barrier_semaphore()
+    pl.semaphore_signal(barrier, inc=1, device_id=(2 * z + 1 - y, ang), device_id_type=MESH)
+    for d in range(1, depth):
+        pl.semaphore_signal(barrier, inc=1, device_id=(2 * z_at(d) + y, ang), device_id_type=MESH)
+    for d in range(1, angles):
+        pl.semaphore_signal(barrier, inc=1, device_id=(cut, angle_at(d)), device_id_type=MESH)
+    pl.semaphore_wait(barrier, depth + angles - 1)
+
+    def angle_copy(d, slot):
+        return pltpu.make_async_remote_copy(
+            src_ref=d_ref.at[0], dst_ref=turn.at[slot],
+            send_sem=as_sem.at[d - 1], recv_sem=ar_sem.at[d - 1],
+            device_id=(cut, angle_at(d)), device_id_type=MESH)
+
+    def z_copy(d, j, slot):
+        return pltpu.make_async_remote_copy(
+            src_ref=turn.at[block_of(z_at(d), j)], dst_ref=held.at[slot, j],
+            send_sem=zs_sem.at[d - 1, j], recv_sem=zr_sem.at[d - 1, j],
+            device_id=(2 * z_at(d) + y, ang), device_id_type=MESH)
+
+    def y_copy(d, slot):
+        return pltpu.make_async_remote_copy(
+            src_ref=held.at[slot], dst_ref=held.at[slot],
+            send_sem=ys_sem.at[d], recv_sem=yr_sem.at[d],
+            device_id=(2 * z + 1 - y, ang), device_id_type=MESH)
+
+    for d in range(1, angles):
+        angle_copy(d, ang).start()
+    turn[ang] = d_ref[0]
+    for d in range(1, angles):
+        angle_copy(d, angle_at(-d)).wait_recv()
+    for d in range(1, depth):
+        for j in range(2):
+            z_copy(d, j, cut).start()
+    for j in range(2):
+        held[cut, j] = turn[block_of(z, j)]
+    y_copy(0, cut).start()
+    for d in range(1, depth):
+        for j in range(2):
+            z_copy(d, j, 2 * z_at(-d) + y).wait_recv()
+        y_copy(d, 2 * z_at(-d) + y).start()
+    for d in range(depth):
+        y_copy(d, 2 * z_at(-d) + 1 - y).wait_recv()
+    out_ref[...] = held[...]
+    for d in range(1, angles):
+        angle_copy(d, ang).wait_send()
+    for d in range(1, depth):
+        for j in range(2):
+            z_copy(d, j, cut).wait_send()
+    for d in range(depth):
+        y_copy(d, 2 * z_at(-d) + y).wait_send()
+
+
+def gather(density, offsets, cuts, angles):
+    _, views, radii = density.shape
+    depth = cuts // 2
+    return pl.pallas_call(
+        functools.partial(gather_kernel, cuts, angles, views, offsets),
+        out_shape=jax.ShapeDtypeStruct((cuts, 2, views, radii), density.dtype),
+        in_specs=[pl.BlockSpec(memory_space=pltpu.VMEM)],
+        out_specs=pl.BlockSpec(memory_space=pltpu.VMEM),
+        scratch_shapes=[
+            pltpu.VMEM((angles, views, radii), density.dtype),
+            pltpu.VMEM((cuts, 2, views, radii), density.dtype),
+            pltpu.SemaphoreType.DMA((angles - 1,)),
+            pltpu.SemaphoreType.DMA((angles - 1,)),
+            pltpu.SemaphoreType.DMA((depth - 1, 2)),
+            pltpu.SemaphoreType.DMA((depth - 1, 2)),
+            pltpu.SemaphoreType.DMA((depth,)),
+            pltpu.SemaphoreType.DMA((depth,)),
+        ],
+        compiler_params=pltpu.CompilerParams(
+            collective_id=1, has_side_effects=True, vmem_limit_bytes=44 * 2**20),
+        name="gather",
+    )(density)
+
+
 def local(density, kernel_blocks):
-    angles_dev = density.shape[1]
-    offsets_dev = kernel_blocks.shape[0]
-    angle_count = lax.axis_size("angle")
+    _, views, radii = density.shape
     cuts = lax.axis_size("cuts")
-    offset_start = lax.axis_index("cuts") * offsets_dev
-    block_steps = offset_start // angles_dev
-    gathered = lax.all_gather(density, "cuts", axis=0, tiled=True)
-    slices, _, radii = gathered.shape
-    full_cycle = lax.all_gather(gathered, "angle", axis=1, tiled=True)
-    doubled = jnp.concatenate([full_cycle, full_cycle[:, :angles_dev]], axis=1)
-    window_start = (lax.axis_index("angle") - block_steps - 1) % angle_count * angles_dev
-    window = lax.dynamic_slice_in_dim(doubled, window_start, 2 * angles_dev, 1)
-    rows = jnp.roll(jnp.swapaxes(window, 0, 1), -1, axis=0).reshape(2 * angles_dev * slices, radii)
-    return project(rows, kernel_blocks, cuts, angles_dev, slices)
+    window = gather(density, kernel_blocks.shape[0], cuts, lax.axis_size("angle"))
+    window = jnp.swapaxes(window.reshape(cuts, 2 * views, radii), 0, 1)
+    rows = jnp.roll(window, -1, axis=0).reshape(2 * views * cuts, radii)
+    return project(rows, kernel_blocks, cuts, views, cuts)
 
 
 def solution(mesh):

time: 127 us -> 80.1 us (0.63)
  blocking collectives: 35.6 us -> 0 us
  Pallas kernels: 48 us -> 77.5 us
  waiting for transfers between devices: 25.1 us -> 0 us
  between operations: 13.5 us -> 0.05 us
  other arithmetic: 1.6 us -> 0.1 us
    all_gather x1 -> x0, blocking collectives: 35.6 us -> none  [local(): gathered = lax.all_gather(density, 'cuts', axis=0, tiled=True)]
    pallas_call x0 -> x1, Pallas kernels: none -> 29.9 us  [gather(): pl.pallas_call(functools.partial(gather_kernel, cuts, angles, views, offs...]
    all_gather x1 -> x0, waiting for transfers between devices: 25.1 us -> none  [local(): full_cycle = lax.all_gather(gathered, 'angle', axis=1, tiled=True)]
    transpose x1 -> x0, other arithmetic: 1.51 us -> none  [local(): jnp.swapaxes(window, 0, 1)]
    slice x3 -> x2, local copies, waits for them, and re-layouts: 1.39 us -> 0.08 us  [local(): rows = jnp.roll(window, -1, axis=0).reshape(2 * views * cuts, radii)]
  transfers between devices with their start and end apart: 1 -> 0, of which waited for: 1 -> 0; matrix products, arithmetic and copies ran while one was open for 0% -> 0% of each run, Pallas kernels for 0% -> 0%
where the time goes in v2:
time: 80.1 us; the launch traced here: 79.9 us
  Pallas kernels  77.5 us (97%)
  local copies, waits for them, and re-layouts  2.27 us (3%)
    pallas_call x1, Pallas kernels, project(): pl.pallas_call(functools.partial(project_kernel, cuts, views, offsets, sl...  47.6 us
    pallas_call x1, Pallas kernels, gather(): pl.pallas_call(functools.partial(gather_kernel, cuts, angles, views, offs...  29.9 us

profile of v2, /device:TPU:0, one launch (start us, length us, event | category | flops | bytes accessed | tf_op | source)
XLA Modules:
  0.0 79.9 jit_solution(5563284334228342345)
XLA Ops:
  0.0 0.0 copy-start
  0.0 0.9 %copy-done = bf16[1,144,256]{2,1,0:T(8,128)(2,1)S(1)} copy-done((bf16[1,144,256]{2,1,0:T(8,128)(2,1)S(1)}, bf16[1,144,256]{2,1,0:T(8,128)(2,1)}, u32[]{:S(2)}) %copy-start) | copy-done | bytes 73752
  0.9 29.9 %gather.1 = bf16[8,2,144,256]{3,2,1,0:T(8,128)(2,1)S(1)} custom-call(bf16[1,144,256]{2,1,0:T(8,128)(2,1)S(1)} %copy-done), custom_call_target="tpu_custom_call" | custom-call | tf_op jit(solution)/shard_map/gather/pallas_call | solution.py:216
  30.8 0.7 copy.5
  31.5 0.1 slice.10
  31.6 0.1 maximum_bitcast_fusion.w_ref
  31.7 47.6 %project.1 = bf16[1,144,384]{2,1,0:T(8,128)(2,1)S(1)} custom-call(bf16[2304,256]{1,0:T(8,128)(2,1)S(1)} %maximum_bitcast_fusion.w_ref, bf16[72,256,384]{2,1,0:T(8,128)(2,1)} %k_ref.1), custom_call_target="tpu_custom_call" | custom-call | flops 16307453952 | bytes 14155776 | tf_op jit(solution)/shard_map/project/pallas_call | solution.py:117
  79.3 0.6 copy.7
  (1 shorter events, 0.0 us)
Async XLA Ops:
  0.0 0.9 %copy-start = (bf16[1,144,256]{2,1,0:T(8,128)(2,1)S(1)}, bf16[1,144,256]{2,1,0:T(8,128)(2,1)}, u32[]{:S(2)}) copy-start(bf16[1,144,256]{2,1,0:T(8,128)(2,1)} %d_ref.1) | copy-start | bytes 221188

commit v3 on v2

--- a/solution.py
+++ b/solution.py
@@ -16,15 +16,15 @@
     return 1
 
 
-def project_kernel(cuts, views, offsets, slices, group, chunk, w_ref, k_ref, out_ref,
+def project_kernel(cuts, views, offsets, slices, group, sizes, w_ref, k_ref, out_ref,
                    k_buf, acc, tmp, part, y_recv, z_recv,
                    k_sem, ys_sem, yr_sem, zs_sem, zr_sem):
     bins = out_ref.shape[-1]
     slabs = bins // 128
     depth = cuts // 2
     steps = offsets // (2 * group)
-    chunks = views // chunk
-    rows = (chunk + 2) * slices
+    chunks = len(sizes)
+    starts = [sum(sizes[:m]) for m in range(chunks)]
     cut = lax.axis_index("cuts")
     ang = lax.axis_index("angle")
     z, y = cut // 2, cut % 2
@@ -45,31 +45,37 @@
 
     def y_copy(m):
         return pltpu.make_async_remote_copy(
-            src_ref=part.at[m, 1 - y], dst_ref=y_recv.at[m],
+            src_ref=part.at[1 - y, :, pl.ds(starts[m], sizes[m])],
+            dst_ref=y_recv.at[:, pl.ds(starts[m], sizes[m])],
             send_sem=ys_sem.at[m], recv_sem=yr_sem.at[m],
             device_id=(2 * z + 1 - y, ang), device_id_type=MESH)
 
     def z_copy(m, d):
         peer = lax.rem(z + d, depth)
         return pltpu.make_async_remote_copy(
-            src_ref=part.at[m, y, peer], dst_ref=z_recv.at[m, d - 1],
+            src_ref=part.at[y, peer, pl.ds(starts[m], sizes[m])],
+            dst_ref=z_recv.at[d - 1, pl.ds(starts[m], sizes[m])],
             send_sem=zs_sem.at[m, d - 1], recv_sem=zr_sem.at[m, d - 1],
             device_id=(2 * peer + y, ang), device_id_type=MESH)
 
     def z_stage(m):
         y_copy(m).wait_recv()
-        part[m, y] += y_recv[m]
+        at = pl.ds(starts[m], sizes[m])
+        part[y, :, at] += y_recv[:, at]
         for d in range(depth - 1, 0, -1):
             z_copy(m, d).start()
 
     for m in range(chunks):
+        chunk, start = sizes[m], starts[m]
+        rows = (chunk + 2) * slices
+
         def body(step, _):
             if m == 0:
                 k_copy(step).wait()
             left, right = [], []
             for n in range(group):
                 pair = step * group + n
-                row = pl.multiple_of((first - 2 * pair + m * chunk) * slices, 16)
+                row = pl.multiple_of((first - 2 * pair + start) * slices, 16)
                 left.append(w_ref[pl.ds(row, rows), :])
                 right.append(jnp.concatenate([k_buf[2 * pair], k_buf[2 * pair + 1]], axis=1))
             product = jnp.dot(jnp.concatenate(left, axis=1), jnp.concatenate(right, axis=0),
@@ -77,31 +83,32 @@
 
             @pl.when(step == 0)
             def _():
-                acc[...] = product
+                acc[:rows] = product
 
             @pl.when(step > 0)
             def _():
-                acc[...] += product
+                acc[:rows] += product
 
             return 0
 
         lax.fori_loop(0, steps, body, 0)
         for b in range(slabs):
-            tmp[b] = (acc[slices:slices + chunk * slices, 128 * b:128 * (b + 1)]
+            tmp[b, :chunk * slices] = (acc[slices:slices + chunk * slices, 128 * b:128 * (b + 1)]
                       + acc[:chunk * slices, bins + 128 * b:bins + 128 * (b + 1)])
         for s in range(slices):
             for b in range(slabs):
-                part[m, s % 2, s // 2, :, 128 * b:128 * (b + 1)] = tmp[b, pl.ds(s, chunk, stride=slices), :]
+                part[s % 2, s // 2, start:start + chunk, 128 * b:128 * (b + 1)] = tmp[b, pl.ds(s, chunk, stride=slices), :]
         y_copy(m).start()
         if m > 0:
             z_stage(m - 1)
     z_stage(chunks - 1)
     for m in range(chunks):
-        total = part[m, y, z]
+        at = pl.ds(starts[m], sizes[m])
+        total = part[y, z, at]
         for d in range(1, depth):
             z_copy(m, d).wait_recv()
-            total += z_recv[m, d - 1]
-        out_ref[0, m * chunk:(m + 1) * chunk, :] = total.astype(out_ref.dtype)
+            total += z_recv[d - 1, at]
+        out_ref[0, at, :] = total.astype(out_ref.dtype)
     for m in range(chunks):
         y_copy(m).wait_send()
         for d in range(1, depth):
@@ -111,11 +118,11 @@
 def project(window, kernel_blocks, cuts, views, slices):
     offsets, radii, bins = kernel_blocks.shape
     group = split_of(offsets // 2, (3, 2))
-    chunk = 48 if views % 48 == 0 else views
-    chunks, depth = views // chunk, cuts // 2
+    sizes = [48] * (views // 48 - 1) + [32, 16] if views % 48 == 0 else [views]
+    chunk, chunks, depth = max(sizes), len(sizes), cuts // 2
     rows = (chunk + 2) * slices
     return pl.pallas_call(
-        functools.partial(project_kernel, cuts, views, offsets, slices, group, chunk),
+        functools.partial(project_kernel, cuts, views, offsets, slices, group, sizes),
         out_shape=jax.ShapeDtypeStruct((1, views, bins), jnp.bfloat16),
         in_specs=[pl.BlockSpec(memory_space=pltpu.VMEM), pl.BlockSpec(memory_space=pl.ANY)],
         out_specs=pl.BlockSpec(memory_space=pltpu.VMEM),
@@ -123,9 +130,9 @@
             pltpu.VMEM((offsets, radii, bins), jnp.bfloat16),
             pltpu.VMEM((rows, 2 * bins), jnp.float32),
             pltpu.VMEM((bins // 128, chunk * slices, 128), jnp.float32),
-            pltpu.VMEM((chunks, 2, depth, chunk, bins), jnp.float32),
-            pltpu.VMEM((chunks, depth, chunk, bins), jnp.float32),
-            pltpu.VMEM((chunks, depth - 1, chunk, bins), jnp.float32),
+            pltpu.VMEM((2, depth, views, bins), jnp.float32),
+            pltpu.VMEM((depth, views, bins), jnp.float32),
+            pltpu.VMEM((depth - 1, views, bins), jnp.float32),
             pltpu.SemaphoreType.DMA((offsets // (2 * group),)),
             pltpu.SemaphoreType.DMA((chunks,)),
             pltpu.SemaphoreType.DMA((chunks,)),

time: 80.1 us -> 77.7 us (0.970)
  Pallas kernels: 77.5 us -> 75.1 us
    pallas_call x1, Pallas kernels: 47.6 us -> 45.2 us  [project(): pl.pallas_call(functools.partial(project_kernel, cuts, views, offsets, sl...]
where the time goes in v3:
time: 77.7 us; the launch traced here: 77.5 us
  Pallas kernels  75.1 us (97%)
  local copies, waits for them, and re-layouts  2.27 us (3%)
    pallas_call x1, Pallas kernels, project(): pl.pallas_call(functools.partial(project_kernel, cuts, views, offsets, sl...  45.2 us
    pallas_call x1, Pallas kernels, gather(): pl.pallas_call(functools.partial(gather_kernel, cuts, angles, views, offs...  29.9 us

profile of v3, /device:TPU:0, one launch (start us, length us, event | category | flops | bytes accessed | tf_op | source)
XLA Modules:
  0.0 77.5 jit_solution(333166580807068887)
XLA Ops:
  0.0 0.0 copy-start
  0.0 0.9 %copy-done = bf16[1,144,256]{2,1,0:T(8,128)(2,1)S(1)} copy-done((bf16[1,144,256]{2,1,0:T(8,128)(2,1)S(1)}, bf16[1,144,256]{2,1,0:T(8,128)(2,1)}, u32[]{:S(2)}) %copy-start) | copy-done | bytes 73752
  0.9 29.9 %gather.1 = bf16[8,2,144,256]{3,2,1,0:T(8,128)(2,1)S(1)} custom-call(bf16[1,144,256]{2,1,0:T(8,128)(2,1)S(1)} %copy-done), custom_call_target="tpu_custom_call" | custom-call | tf_op jit(solution)/shard_map/gather/pallas_call | solution.py:223
  30.8 0.7 copy.5
  31.5 0.1 slice.10
  31.6 0.1 maximum_bitcast_fusion.w_ref
  31.7 45.2 %project.1 = bf16[1,144,384]{2,1,0:T(8,128)(2,1)S(1)} custom-call(bf16[2304,256]{1,0:T(8,128)(2,1)S(1)} %maximum_bitcast_fusion.w_ref, bf16[72,256,384]{2,1,0:T(8,128)(2,1)} %k_ref.1), custom_call_target="tpu_custom_call" | custom-call | flops 16307453952 | bytes 14155776 | tf_op jit(solution)/shard_map/project/pallas_call | solution.py:124
  76.9 0.6 copy.7
  (1 shorter events, 0.0 us)
Async XLA Ops:
  0.0 0.9 %copy-start = (bf16[1,144,256]{2,1,0:T(8,128)(2,1)S(1)}, bf16[1,144,256]{2,1,0:T(8,128)(2,1)}, u32[]{:S(2)}) copy-start(bf16[1,144,256]{2,1,0:T(8,128)(2,1)} %d_ref.1) | copy-start | bytes 221188

commit v4 on v3

--- a/solution.py
+++ b/solution.py
@@ -184,10 +184,16 @@
             send_sem=zs_sem.at[d - 1, j], recv_sem=zr_sem.at[d - 1, j],
             device_id=(2 * z_at(d) + y, ang), device_id_type=MESH)
 
-    def y_copy(d, slot):
-        return pltpu.make_async_remote_copy(
-            src_ref=held.at[slot], dst_ref=held.at[slot],
-            send_sem=ys_sem.at[d], recv_sem=yr_sem.at[d],
+    trim = min(offsets, views - offsets) // 16 * 16 if views % 16 == 0 else 0
+
+    def y_copy(d, slot, to_y, short):
+        if short:
+            ref = held.at[slot, to_y, pl.ds(pl.multiple_of((1 - to_y) * trim, 16), views - trim)]
+        else:
+            ref = held.at[slot, 1 - to_y]
+        return pltpu.make_async_remote_copy(
+            src_ref=ref, dst_ref=ref,
+            send_sem=ys_sem.at[d, short], recv_sem=yr_sem.at[d, short],
             device_id=(2 * z + 1 - y, ang), device_id_type=MESH)
 
     for d in range(1, angles):
@@ -200,13 +206,20 @@
             z_copy(d, j, cut).start()
     for j in range(2):
         held[cut, j] = turn[block_of(z, j)]
-    y_copy(0, cut).start()
+    for short in range(2):
+        y_copy(0, cut, 1 - y, short).start()
     for d in range(1, depth):
         for j in range(2):
             z_copy(d, j, 2 * z_at(-d) + y).wait_recv()
-        y_copy(d, 2 * z_at(-d) + y).start()
+        for short in range(2):
+            y_copy(d, 2 * z_at(-d) + y, 1 - y, short).start()
     for d in range(depth):
-        y_copy(d, 2 * z_at(-d) + 1 - y).wait_recv()
+        slot = 2 * z_at(-d) + 1 - y
+        if trim:
+            rest = pl.ds(pl.multiple_of(y * (views - trim), 16), trim)
+            held[slot, y, rest, :] = jnp.zeros((trim, held.shape[-1]), held.dtype)
+        for short in range(2):
+            y_copy(d, slot, y, short).wait_recv()
     out_ref[...] = held[...]
     for d in range(1, angles):
         angle_copy(d, ang).wait_send()
@@ -214,7 +227,8 @@
         for j in range(2):
             z_copy(d, j, cut).wait_send()
     for d in range(depth):
-        y_copy(d, 2 * z_at(-d) + y).wait_send()
+        for short in range(2):
+            y_copy(d, 2 * z_at(-d) + y, 1 - y, short).wait_send()
 
 
 def gather(density, offsets, cuts, angles):
@@ -232,8 +246,8 @@
             pltpu.SemaphoreType.DMA((angles - 1,)),
             pltpu.SemaphoreType.DMA((depth - 1, 2)),
             pltpu.SemaphoreType.DMA((depth - 1, 2)),
-            pltpu.SemaphoreType.DMA((depth,)),
-            pltpu.SemaphoreType.DMA((depth,)),
+            pltpu.SemaphoreType.DMA((depth, 2)),
+            pltpu.SemaphoreType.DMA((depth, 2)),
         ],
         compiler_params=pltpu.CompilerParams(
             collective_id=1, has_side_effects=True, vmem_limit_bytes=44 * 2**20),

time: 77.7 us -> 76.3 us (0.982)
  Pallas kernels: 75.1 us -> 73.8 us
    pallas_call x1, Pallas kernels: 29.9 us -> 28.6 us  [gather(): pl.pallas_call(functools.partial(gather_kernel, cuts, angles, views, offs...]
where the time goes in v4:
time: 76.3 us; the launch traced here: 76.2 us
  Pallas kernels  73.8 us (97%)
  local copies, waits for them, and re-layouts  2.27 us (3%)
    pallas_call x1, Pallas kernels, project(): pl.pallas_call(functools.partial(project_kernel, cuts, views, offsets, sl...  45.2 us
    pallas_call x1, Pallas kernels, gather(): pl.pallas_call(functools.partial(gather_kernel, cuts, angles, views, offs...  28.6 us
    unnamed x3, local copies, waits for them, and re-layouts  1.53 us

profile of v4, /device:TPU:0, one launch (start us, length us, event | category | flops | bytes accessed | tf_op | source)
XLA Modules:
  0.0 76.2 jit_solution(4776474817599012840)
XLA Ops:
  0.0 0.0 copy-start
  0.0 0.9 %copy-done = bf16[1,144,256]{2,1,0:T(8,128)(2,1)S(1)} copy-done((bf16[1,144,256]{2,1,0:T(8,128)(2,1)S(1)}, bf16[1,144,256]{2,1,0:T(8,128)(2,1)}, u32[]{:S(2)}) %copy-start) | copy-done | bytes 73752
  0.9 28.6 %gather.1 = bf16[8,2,144,256]{3,2,1,0:T(8,128)(2,1)S(1)} custom-call(bf16[1,144,256]{2,1,0:T(8,128)(2,1)S(1)} %copy-done), custom_call_target="tpu_custom_call" | custom-call | tf_op jit(solution)/shard_map/gather/pallas_call | solution.py:237
  29.5 0.7 copy.5
  30.1 0.1 slice.10
  30.2 0.1 maximum_bitcast_fusion.w_ref
  30.3 45.2 %project.1 = bf16[1,144,384]{2,1,0:T(8,128)(2,1)S(1)} custom-call(bf16[2304,256]{1,0:T(8,128)(2,1)S(1)} %maximum_bitcast_fusion.w_ref, bf16[72,256,384]{2,1,0:T(8,128)(2,1)} %k_ref.1), custom_call_target="tpu_custom_call" | custom-call | flops 16307453952 | bytes 14155776 | tf_op jit(solution)/shard_map/project/pallas_call | solution.py:124
  75.5 0.6 copy.7
  (1 shorter events, 0.0 us)
Async XLA Ops:
  0.0 0.9 %copy-start = (bf16[1,144,256]{2,1,0:T(8,128)(2,1)S(1)}, bf16[1,144,256]{2,1,0:T(8,128)(2,1)}, u32[]{:S(2)}) copy-start(bf16[1,144,256]{2,1,0:T(8,128)(2,1)} %d_ref.1) | copy-start | bytes 221188
